TPU v7x, 32 devices: a whole 2x2x4 slice. The times are simulated.
32 devices in a mesh: parts: 2 (over y), users: 16 (over z, x, core).
Axes of the slice: x: 2, y: 2, z: 4, core: 2. Of those that a mesh axis runs over, the one named last changes fastest.
Arguments:
- candidates: bfloat16 [512, 512], P(('parts', 'users')), parts along dimension 0, may hold values from -6 to 6
- candidate_user: int32 [512], P(('parts', 'users')), parts along dimension 0, may hold values from 0 to 7
- events: bfloat16 [65536, 512], P(('parts', 'users')), parts along dimension 0, may hold values from -6 to 6
- event_user: int32 [65536], P(('parts', 'users')), parts along dimension 0, may hold values from 0 to 7, never falling along the last dimension, each value on 1 to 12288 neighbouring positions
- event_mask: int32 [65536], P(('parts', 'users')), parts along dimension 0, may hold values 0 or 1
- query_weight: bfloat16 [512, 512], replicated, may hold values from -0.25 to 0.25
- key_weight: bfloat16 [512, 512], replicated, may hold values from -0.25 to 0.25
- value_weight: bfloat16 [512, 512], replicated, may hold values from -2 to 2
- gate_weight: bfloat16 [512, 512], replicated, may hold values from -0.25 to 0.25
- output_weight: bfloat16 [512, 512], replicated, may hold values from -0.25 to 0.25
Outputs:
- candidate_out: bfloat16 [512, 512], P(('parts', 'users')), parts along dimension 0
There are 2 independent parts, one for each index of `parts`. A program takes and returns all parts, laid end to end along the dimension named above; an argument that names none is the same for every part. Nothing has to cross between parts.
Inputs may be any that keep to these rules, and one draw needn't show every extreme that they name: event_user never falls along the events; each user's events form one run of at most 12288 slots.
All inputs are finite; a program needn't handle non-finite values. No bound on the sum of `event_mask` on one device may be relied on, other than what follows from the above.
Results may differ from a plain program's by a relative error of at most 0.0044.
Values may be sent and summed in bfloat16 or wider, within the bound.
A program may use at most 64 MiB of HBM per device.

v0:
```python
import math

import jax
import jax.numpy as jnp
from jax import lax
from jax.sharding import PartitionSpec as P

HEADS = 4


def per_device(
    candidates,
    candidate_user,
    events,
    event_user,
    event_mask,
    query_weight,
    key_weight,
    value_weight,
    gate_weight,
    output_weight,
):
    own_count = candidates.shape[0]
    model_width = candidates.shape[1]
    head_count = HEADS
    head_size = model_width // head_count
    score_scale = 1.0 / math.sqrt(head_size)
    queries = jnp.dot(candidates, query_weight, preferred_element_type=jnp.float32).astype(
        jnp.bfloat16
    )
    gate_values = jax.nn.silu(jnp.dot(candidates, gate_weight, preferred_element_type=jnp.float32))
    key_rows = jnp.dot(events, key_weight, preferred_element_type=jnp.float32).astype(jnp.bfloat16)
    value_rows = jnp.dot(events, value_weight, preferred_element_type=jnp.float32).astype(
        jnp.bfloat16
    )
    event_count = key_rows.shape[0]
    key_heads = key_rows.reshape(event_count, head_count, head_size)
    value_heads = value_rows.reshape(event_count, head_count, head_size)
    valid_events = event_mask.astype(jnp.float32)
    all_queries, all_users = (
        lax.all_gather(queries, "users", axis=0, tiled=True),
        lax.all_gather(candidate_user, "users", axis=0, tiled=True),
    )

    def one_block(block_pair):
        query_block, user_block = block_pair
        scores = (
            jnp.einsum("chd,ehd->hce", query_block, key_heads, preferred_element_type=jnp.float32)
            * score_scale
        )
        same_user = (user_block[:, None] == event_user[None, :]).astype(jnp.float32) * valid_events[
            None, :
        ]
        attn_weights = (jax.nn.silu(scores) * same_user[None]).astype(jnp.bfloat16)
        mixed_rows = jnp.einsum(
            "hce,ehd->chd", attn_weights, value_heads, preferred_element_type=jnp.float32
        )
        return mixed_rows.reshape(query_block.shape[0], model_width)

    row_count = own_count * lax.axis_size("users")
    row_block = math.gcd(row_count, 512)
    query_part = all_queries
    query_part = query_part.reshape(row_count // row_block, row_block, head_count, head_size)
    user_part = all_users.reshape(row_count // row_block, row_block)
    summed = lax.psum_scatter(
        lax.map(one_block, (query_part, user_part)).reshape(row_count, model_width),
        "users",
        scatter_dimension=0,
        tiled=True,
    )
    mean_row = jnp.mean(summed, axis=1, keepdims=True)
    centred = summed - mean_row
    var_row = jnp.mean(centred * centred, axis=1, keepdims=True)
    normed = centred / jnp.sqrt(var_row + 1e-05)
    gated_rows = (normed * gate_values).astype(jnp.bfloat16)
    result = candidates.astype(jnp.float32) + jnp.dot(
        gated_rows, output_weight, preferred_element_type=jnp.float32
    )
    return result.astype(jnp.bfloat16)


def solution(mesh):
    in_specs = (
        P(("parts", "users"), None),
        P(("parts", "users")),
        P(("parts", "users"), None),
        P(("parts", "users")),
        P(("parts", "users")),
        P(),
        P(),
        P(),
        P(),
        P(),
    )
    out_specs = P(("parts", "users"), None)
    return jax.shard_map(
        per_device, mesh=mesh, in_specs=in_specs, out_specs=out_specs, check_vma=False
    )
```

profile of v0, /device:TPU:0, one launch (start us, length us, event | category | flops | bytes accessed | tf_op | source)
XLA Modules:
  0.0 126.2 jit_solution(15532757817765731174)
XLA Ops:
  6.5 0.0 copy-start
  6.5 0.0 reduce-scatter.2.cloned.1.call-start
  6.5 1.4 %dynamic-slice.1 = u32[1]{0:T(128)} dynamic-slice(u32[32]{0:T(128)} %constant.34, u32[]{:T(128)S(6)} %add.28), dynamic_slice_sizes={1} | dynamic-slice | bytes 12
  8.6 0.9 dynamic-update-slice
  9.4 13.7 %all-reduce = s32[256]{0:T(256)S(1)} all-reduce(s32[256]{0:T(256)S(1)} %dynamic-update-slice), channel_id=1, replica_groups=mesh['parts'=2,'users'=16] {'users'}, use_global_device_ids=true, to_apply=%add | all-reduce | flops 256 | bytes 2048
  23.1 0.7 convert_element_type.31
  23.8 1.2 convolution_convert_fusion.2
  25.1 18.7 %all_gather.6 = bf16[256,512]{1,0:T(8,128)(2,1)S(1)} all-gather(bf16[16,512]{1,0:T(8,128)(2,1)S(1)} %convolution_convert_fusion.2), channel_id=1, replica_groups=mesh['parts'=2,'users'=16] {'users'}, dimensions={0}, use_global_device_ids=true | all-gather | bytes 278528 | tf_op jit(solution)/shard_map/all_gather | solution.py:41
  43.7 0.0 copy-done
  43.7 0.0 copy-start.5
  43.7 3.7 %convolution_convert_fusion = bf16[2048,512]{0,1:T(8,128)(2,1)} fusion(bf16[2048,512]{1,0:T(8,128)(2,1)S(1)} %copy-done, bf16[512,512]{1,0:T(8,128)(2,1)} %param.16), kind=kOutput, calls=%fused_computation.1 | convolution fusion | flops 1074790400 | bytes 4718592 | tf_op jit(solution)/shard_map/dot_general | solution.py:32
  47.4 0.0 copy-done.5
  47.4 0.0 copy-start.4
  47.4 2.7 %convolution_convert_fusion.1 = bf16[2048,512]{0,1:T(8,128)(2,1)} fusion(bf16[2048,512]{1,0:T(8,128)(2,1)S(1)} %copy-done, bf16[512,512]{1,0:T(8,128)(2,1)S(1)} %copy-done.5), kind=kOutput, calls=%fused_computation.2 | convolution fusion | flops 1074790400 | bytes 4718592 | tf_op jit(solution)/shard_map/dot_general | solution.py:33
  50.1 0.0 copy-done.4
  50.1 1.5 %compare_select_fusion = f32[256,2048]{1,0:T(8,128)} fusion(f32[2048]{0:T(1024)S(1)} %convert_element_type.31, s32[2048]{0:T(1024)S(1)} %copy-done.4, s32[256]{0:T(256)S(1)} %all-reduce), kind=kLoop, calls=%fused_computation.3 | loop fusion | flops 1048576 | bytes 2114560 | tf_op jit(solution)/shard_map/while/body/eval_jaxpr/mul | solution.py:51
  51.6 0.0 copy-start.1
  51.6 0.0 copy-start.2
  51.6 0.0 copy-start.3
  51.6 8.2 %fusion = f32[4,128,256]{2,1,0:T(8,128)} fusion(bf16[2048,4,128]{0,2,1:T(8,128)(2,1)} %bitcast.28, bf16[2048,4,128]{0,2,1:T(8,128)(2,1)} %bitcast.27, f32[256,2048]{1,0:T(8,128)} %compare_select_fusion, bf16[256,512]{1,0:T(8,128)(2,1)S(1)} %all_gather.6), kind=kOutput, calls=%fused_computation.4 | convolution fusion | flops 1088421888 | bytes 7077888 | tf_op jit(solution)/shard_map/while/body/eval_jaxpr/hce,ehd->chd/dot_general | solution.py:55
  59.8 2.0 %copy.13 = f32[256,512]{1,0:T(8,128)} copy(f32[256,512]{0,1:T(8,128)} %bitcast.26) | data formatting | bytes 1048576 | tf_op jit(solution)/shard_map/reshape | solution.py:66
  61.9 0.0 reduce-scatter.2.cloned.1.call-update
  61.9 53.9 %reduce-scatter.2.cloned.1.call-done = f32[16,512]{1,0:T(8,128)} async-done(((f32[256,512]{1,0:T(8,128)}), f32[16,512]{1,0:T(8,128)}) %reduce-scatter.2.cloned.1.call-update) | async-done | bytes 32784 | tf_op jit(solution)/shard_map/reduce_scatter | solution.py:65
  115.8 0.9 reduce_sum.18
  116.7 0.9 multiply_reduce_fusion
  117.6 0.0 copy-done.1
  117.6 0.0 copy-done.2
  117.6 0.0 copy-done.3
  117.6 1.7 %fusion.1 = bf16[16,512]{1,0:T(8,128)(2,1)} fusion(bf16[512,512]{1,0:T(8,128)(2,1)S(1)} %copy-done.1, bf16[16,512]{1,0:T(8,128)(2,1)S(1)} %copy-done.3, f32[16,512]{1,0:T(8,128)} %reduce-scatter.2.cloned.1.call-done, f32[16]{0:T(128)S(1)} %add_sqrt_fusion, f32[16]{0:T(128)S(1)} %broadcast_multiply_fusion, bf16[512,512]{1,0:T(8,128)(2,1)S(1)} %copy-done.2), kind=kOutput, calls=%fused_computation.6 | convolution fusion | flops 16867328 | bytes 1114240 | tf_op jit(solution)/shard_map/dot_general | solution.py:76
  (3 shorter events, 0.0 us)
Async XLA Ops:
  6.5 37.2 %copy-start = (bf16[2048,512]{1,0:T(8,128)(2,1)S(1)}, bf16[2048,512]{1,0:T(8,128)(2,1)}, u32[]{:S(2)}) copy-start(bf16[2048,512]{1,0:T(8,128)(2,1)} %param.12) | copy-start | bytes 6291460
  6.5 109.2 %reduce-scatter.2.cloned.1.call-start = ((), (), s32[]{:S(2)}) async-start(), calls=%async_computation.1 | async-start | bytes 557056 | tf_op jit(solution)/shard_map/reduce_scatter | solution.py:65
  43.7 3.7 %copy-start.5 = (bf16[512,512]{1,0:T(8,128)(2,1)S(1)}, bf16[512,512]{1,0:T(8,128)(2,1)}, u32[]{:S(2)}) copy-start(bf16[512,512]{1,0:T(8,128)(2,1)} %param.17) | copy-start | bytes 1572868
  47.4 2.7 %copy-start.4 = (s32[2048]{0:T(1024)S(1)}, s32[2048]{0:T(1024)}, u32[]{:S(2)}) copy-start(s32[2048]{0:T(1024)} %param.13) | copy-start | bytes 24580
  51.6 66.0 %copy-start.1 = (bf16[512,512]{1,0:T(8,128)(2,1)S(1)}, bf16[512,512]{1,0:T(8,128)(2,1)}, u32[]{:S(2)}) copy-start(bf16[512,512]{1,0:T(8,128)(2,1)} %param.19) | copy-start | bytes 1572868
  51.6 66.0 %copy-start.2 = (bf16[512,512]{1,0:T(8,128)(2,1)S(1)}, bf16[512,512]{1,0:T(8,128)(2,1)}, u32[]{:S(2)}) copy-start(bf16[512,512]{1,0:T(8,128)(2,1)} %param.18) | copy-start | bytes 1572868
  51.6 66.0 %copy-start.3 = (bf16[16,512]{1,0:T(8,128)(2,1)S(1)}, bf16[16,512]{1,0:T(8,128)(2,1)}, u32[]{:S(2)}) copy-start(bf16[16,512]{1,0:T(8,128)(2,1)} %param.10) | copy-start | bytes 49156
Sparse Core Ops, SparseCore 0:
  62.0 53.7 reduce-scatter.1
where the time goes:
time: 127 us; the launch traced here: 126 us
  waiting for transfers between devices  53.9 us (42%)
  blocking collectives  32.4 us (26%)
  matrix products  17.5 us (14%)
  between operations  14.1 us (11%)
  local copies, waits for them, and re-layouts  4.3 us (3%)
  other arithmetic  4.07 us (3%)
    reduce_scatter x1, waiting for transfers between devices, per_device(): lax.psum_scatter(lax.map(one_block, (query_part, user_part)).reshape(row_...  53.9 us
    all_gather x1, blocking collectives, per_device(): lax.all_gather(queries, 'users', axis=0, tiled=True)  18.7 us
    unnamed x1, blocking collectives  13.7 us
    dot_general x1, matrix products, one_block(): jnp.einsum('hce,ehd->chd', attn_weights, value_heads, preferred_element_t...  8.2 us
    dot_general x1, matrix products, per_device(): jnp.dot(events, key_weight, preferred_element_type=jnp.float32)  3.69 us
    dot_general x1, matrix products, per_device(): jnp.dot(events, value_weight, preferred_element_type=jnp.float32)  2.65 us
  transfers between devices with their start and end apart: 1, of which 1 were waited for; matrix products, arithmetic and copies ran while one was open for 0% of the time, Pallas kernels for 0%

commit v1 on v0

v1 whole, which is shorter than its diff:
```python
import functools
import math

import jax
import jax.numpy as jnp
from jax import lax
from jax.experimental import pallas as pl
from jax.experimental.pallas import tpu as pltpu
from jax.sharding import PartitionSpec as P

HEADS = 4
LANES = 128
FAR = -(2.0**60)
LINK = jnp.float32
F32 = jnp.float32
BF16 = jnp.bfloat16


def divisor(total, wanted):
    return math.gcd(total, wanted)


def kernel(
    n,
    cand_hbm,
    cuser_hbm,
    ev_hbm,
    euser_hbm,
    emask_hbm,
    wq_hbm,
    wk_hbm,
    wv_hbm,
    wg_hbm,
    wo_hbm,
    out_ref,
    cand,
    cuser,
    ev,
    euser,
    emask,
    wq,
    wk,
    wv,
    wg,
    wo,
    q_all,
    keys,
    vals,
    gate,
    part,
    sib,
    chip,
    land,
    in_sem,
    ev_sem,
    q_send,
    q_recv,
    f_sem,
    s_send,
    s_recv,
    r_send,
    r_recv,
):
    chips = n // 2
    rows, width = cand.shape
    dh = width // HEADS
    events = ev.shape[0]
    chunk = divisor(events, 512)
    ev_chunks = events // chunk
    half_scale = 0.5 / math.sqrt(dh)

    me = lax.axis_index("users")
    k = me // 2
    c = lax.rem(me, 2)
    other = 1 - c
    sibling = {"users": k * 2 + other}

    def peer_of(i):
        return lax.rem(k + i, chips)

    small = [
        (cand_hbm, cand),
        (cuser_hbm, cuser),
        (wq_hbm, wq),
        (euser_hbm, euser),
        (emask_hbm, emask),
        (wk_hbm, wk),
        (wv_hbm, wv),
        (wg_hbm, wg),
        (wo_hbm, wo),
    ]
    copies = [pltpu.make_async_copy(s, d, in_sem.at[i]) for i, (s, d) in enumerate(small)]
    ev_copies = [
        pltpu.make_async_copy(
            ev_hbm.at[pl.ds(j * chunk, chunk)], ev.at[pl.ds(j * chunk, chunk)], ev_sem.at[j]
        )
        for j in range(ev_chunks)
    ]

    barrier = pltpu.get_barrier_semaphore()

    @pl.loop(1, chips)
    def _(i):
        pl.semaphore_signal(barrier, inc=1, device_id={"users": peer_of(i) * 2 + c})

    pl.semaphore_signal(barrier, inc=1, device_id=sibling)

    for copy in copies[:6]:
        copy.start()
    for copy in ev_copies:
        copy.start()
    for copy in copies[6:]:
        copy.start()

    for copy in copies[:3]:
        copy.wait()
    queries = jnp.dot(cand[...], wq[...], preferred_element_type=F32).astype(BF16)
    diagonal = lax.broadcasted_iota(jnp.int32, (rows, rows), 0) == lax.broadcasted_iota(
        jnp.int32, (rows, rows), 1
    )
    user_col = jnp.sum(
        jnp.where(diagonal, jnp.broadcast_to(cuser[...].astype(F32), (rows, rows)), 0.0),
        axis=1,
        keepdims=True,
    )
    lane_ids = lax.broadcasted_iota(jnp.int32, (rows, LANES), 1).astype(F32)
    one_hot = jnp.where(lane_ids == user_col, 1.0, 0.0).astype(BF16)
    mine = c * chips + k
    q_all[mine, :, pl.ds(0, width)] = queries
    q_all[mine, :, pl.ds(width, LANES)] = one_hot

    pl.semaphore_wait(barrier, chips)

    def q_copy(i):
        peer = peer_of(i)
        return pltpu.make_async_remote_copy(
            src_ref=q_all.at[mine],
            dst_ref=q_all.at[mine],
            send_sem=q_send.at[peer],
            recv_sem=q_recv.at[k],
            device_id={"users": peer * 2 + c},
        )

    def q_arrival(i):
        peer = peer_of(i)
        slot = q_all.at[c * chips + peer]
        return pltpu.make_async_remote_copy(
            src_ref=slot,
            dst_ref=slot,
            send_sem=q_send.at[peer],
            recv_sem=q_recv.at[peer],
            device_id={"users": peer * 2 + c},
        )

    @pl.loop(1, chips)
    def _(i):
        q_copy(i).start()

    copies[3].wait()
    copies[4].wait()
    for j in range(ev_chunks):
        at = pl.ds(j * chunk, chunk)
        eff = jnp.where(emask[:, at] == 1, euser[:, at], -1)
        ids = lax.broadcasted_iota(jnp.int32, (LANES, chunk), 0)
        miss = jnp.where(ids == eff, 0.0, FAR)
        miss = miss.T.astype(BF16)
        for h in range(HEADS):
            keys[h, at, pl.ds(dh, LANES)] = miss

    copies[5].wait()
    for j in range(ev_chunks):
        at = pl.ds(j * chunk, chunk)
        ev_copies[j].wait()
        rows_k = jnp.dot(ev[at, :], wk[...], preferred_element_type=F32).astype(BF16)
        for h in range(HEADS):
            keys[h, at, pl.ds(0, dh)] = rows_k[:, h * dh : (h + 1) * dh]

    @pl.loop(1, chips)
    def _(i):
        q_arrival(i).wait_recv()

    def forward(core):
        block = q_all.at[pl.ds(core * chips, chips)]
        return pltpu.make_async_remote_copy(
            src_ref=block,
            dst_ref=block,
            send_sem=f_sem.at[0],
            recv_sem=f_sem.at[1],
            device_id=sibling,
        )

    forward(c).start()

    copies[6].wait()
    for j in range(ev_chunks):
        at = pl.ds(j * chunk, chunk)
        vals[at, :] = jnp.dot(ev[at, :], wv[...], preferred_element_type=F32).astype(BF16)

    copies[7].wait()
    pre = 0.5 * jnp.dot(cand[...], wg[...], preferred_element_type=F32)
    gate[...] = pre + pre * jnp.tanh(pre)
    copies[8].wait()

    forward(other).wait_recv()

    total = n * rows
    block = divisor(total, 256)
    slots = block // rows

    def attention(h, b):
        at_slots = pl.ds(b * slots, slots)
        q = q_all[at_slots].reshape(block, width + LANES)
        q = jnp.concatenate([q[:, h * dh : (h + 1) * dh], q[:, width:]], axis=1)
        acc = None
        for j in range(ev_chunks):
            at = pl.ds(j * chunk, chunk)
            raw = lax.dot_general(
                q, keys[h, at, :], (((1,), (1,)), ((), ())), preferred_element_type=F32
            )
            s = raw * half_scale
            attn = (s + s * jnp.tanh(s)).astype(BF16)
            term = jnp.dot(attn, vals[at, pl.ds(h * dh, dh)], preferred_element_type=F32)
            acc = term if acc is None else acc + term
        part[h, at_slots] = acc.reshape(slots, rows, dh)

    def to_sibling(h, core):
        return pltpu.make_async_remote_copy(
            src_ref=part.at[h, pl.ds(core * chips, chips)],
            dst_ref=sib.at[h],
            send_sem=s_send.at[h],
            recv_sem=s_recv.at[h],
            device_id=sibling,
        )

    def to_chip(h, i):
        peer = peer_of(i)
        return pltpu.make_async_remote_copy(
            src_ref=chip.at[h, peer],
            dst_ref=land.at[h, k],
            send_sem=r_send.at[h, peer],
            recv_sem=r_recv.at[h, k],
            device_id={"users": peer * 2 + c},
        )

    def from_chip(h, i):
        peer = peer_of(i)
        return pltpu.make_async_remote_copy(
            src_ref=chip.at[h, peer],
            dst_ref=land.at[h, peer],
            send_sem=r_send.at[h, peer],
            recv_sem=r_recv.at[h, peer],
            device_id={"users": peer * 2 + c},
        )

    def pass_on(h):
        to_sibling(h, other).wait_recv()
        both = part[h, pl.ds(c * chips, chips)] + sib[h]
        chip[h] = both.astype(LINK)

        @pl.loop(1, chips)
        def _(i):
            to_chip(h, i).start()

        land[h, k] = chip[h, k]

    for h in range(HEADS):
        if total == block:
            attention(h, 0)
        else:
            pl.loop(0, total // block)(functools.partial(attention, h))
        to_sibling(h, other).start()
        if h:
            pass_on(h - 1)
    pass_on(HEADS - 1)

    sums = []
    for h in range(HEADS):

        @pl.loop(1, chips)
        def _(i):
            from_chip(h, i).wait_recv()

        sums.append(jnp.sum(land[h].astype(F32), axis=0))
    summed = jnp.concatenate(sums, axis=1)
    mean = jnp.mean(summed, axis=1, keepdims=True)
    centred = summed - mean
    var = jnp.mean(centred * centred, axis=1, keepdims=True)
    normed = centred / jnp.sqrt(var + 1e-5)
    gated = (normed * gate[...]).astype(BF16)
    result = cand[...].astype(F32) + jnp.dot(gated, wo[...], preferred_element_type=F32)
    out_ref[...] = result.astype(out_ref.dtype)

    @pl.loop(1, chips)
    def _(i):
        q_copy(i).wait_send()

    forward(c).wait_send()
    for h in range(HEADS):
        to_sibling(h, other).wait_send()

        @pl.loop(1, chips)
        def _(i):
            to_chip(h, i).wait_send()


def per_device(
    n,
    candidates,
    candidate_user,
    events,
    event_user,
    event_mask,
    query_weight,
    key_weight,
    value_weight,
    gate_weight,
    output_weight,
):
    rows, width = candidates.shape
    count = events.shape[0]
    chips = n // 2
    dh = width // HEADS
    chunks = count // divisor(count, 512)
    square = pltpu.VMEM((width, width), BF16)
    dma = pltpu.SemaphoreType.DMA
    return pl.pallas_call(
        functools.partial(kernel, n),
        out_shape=jax.ShapeDtypeStruct((rows, width), BF16),
        in_specs=[pl.BlockSpec(memory_space=pl.ANY)] * 10,
        out_specs=pl.BlockSpec(memory_space=pltpu.VMEM),
        scratch_shapes=[
            pltpu.VMEM((rows, width), BF16),
            pltpu.VMEM((1, rows), jnp.int32),
            pltpu.VMEM((count, width), BF16),
            pltpu.VMEM((1, count), jnp.int32),
            pltpu.VMEM((1, count), jnp.int32),
            square,
            square,
            square,
            square,
            square,
            pltpu.VMEM((n, rows, width + LANES), BF16),
            pltpu.VMEM((HEADS, count, dh + LANES), BF16),
            pltpu.VMEM((count, width), BF16),
            pltpu.VMEM((rows, width), F32),
            pltpu.VMEM((HEADS, n, rows, dh), F32),
            pltpu.VMEM((HEADS, chips, rows, dh), F32),
            pltpu.VMEM((HEADS, chips, rows, dh), LINK),
            pltpu.VMEM((HEADS, chips, rows, dh), LINK),
            dma((9,)),
            dma((chunks,)),
            dma((chips,)),
            dma((chips,)),
            dma((2,)),
            dma((HEADS,)),
            dma((HEADS,)),
            dma((HEADS, chips)),
            dma((HEADS, chips)),
        ],
        compiler_params=pltpu.CompilerParams(
            collective_id=0, has_side_effects=True, vmem_limit_bytes=56 * 2**20
        ),
    )(
        candidates,
        candidate_user.reshape(1, rows),
        events,
        event_user.reshape(1, count),
        event_mask.reshape(1, count),
        query_weight,
        key_weight,
        value_weight,
        gate_weight,
        output_weight,
    )


def solution(mesh):
    spread = ("parts", "users")
    in_specs = (P(spread, None), P(spread), P(spread, None), P(spread), P(spread)) + (P(),) * 5
    return jax.shard_map(
        functools.partial(per_device, mesh.shape["users"]),
        mesh=mesh,
        in_specs=in_specs,
        out_specs=P(spread, None),
        check_vma=False,
    )
```

time: 127 us -> 26.5 us (0.21)
  waiting for transfers between devices: 53.9 us -> 0 us
  blocking collectives: 32.4 us -> 0 us
  Pallas kernels: 0 us -> 24.9 us
  matrix products: 17.5 us -> 0 us
  between operations: 14.1 us -> 0.01 us
  other arithmetic: 4.07 us -> 0 us
  local copies, waits for them, and re-layouts: 4.3 us -> 1.32 us
    reduce_scatter x1 -> x0, waiting for transfers between devices: 53.9 us -> none  [per_device(): lax.psum_scatter(lax.map(one_block, (query_part, user_part)).reshape(row_...]
    pallas_call x0 -> x1, Pallas kernels: none -> 24.9 us  [per_device(): pl.pallas_call(functools.partial(kernel, n), out_shape=jax.ShapeDtypeStru...]
    all_gather x1 -> x0, blocking collectives: 18.7 us -> none  [per_device(): lax.all_gather(queries, 'users', axis=0, tiled=True)]
    dot_general x5 -> x0, matrix products: 17.5 us -> none  [the longest x1 8.2 us: one_block(): jnp.einsum('hce,ehd->chd', attn_weights, value_heads, preferred_element_t...]
    unnamed x1 -> x0, blocking collectives: 13.7 us -> none
    reshape x1 -> x0, local copies, waits for them, and re-layouts: 2.03 us -> none  [per_device(): lax.map(one_block, (query_part, user_part)).reshape(row_count, model_width)]
    reduce_sum x2 -> x0, other arithmetic: 1.82 us -> none  [the longest x1 0.94 us: per_device(): var_row = jnp.mean(centred * centred, axis=1, keepdims=True)]
    mul x1 -> x0, other arithmetic: 1.54 us -> none  [one_block(): (user_block[:, None] == event_user[None, :]).astype(jnp.float32)]
  transfers between devices with their start and end apart: 1 -> 0, of which waited for: 1 -> 0; matrix products, arithmetic and copies ran while one was open for 0% -> 0% of each run, Pallas kernels for 0% -> 0%
where the time goes in v1:
time: 26.5 us; the launch traced here: 26.2 us
  Pallas kernels  24.9 us (94%)
  local copies, waits for them, and re-layouts  1.32 us (5%)
    pallas_call x1, Pallas kernels, per_device(): pl.pallas_call(functools.partial(kernel, n), out_shape=jax.ShapeDtypeStru...  24.9 us
    unnamed x1, local copies, waits for them, and re-layouts  1.32 us

profile of v1, /device:TPU:0, one launch (start us, length us, event | category | flops | bytes accessed | tf_op | source)
XLA Modules:
  0.0 26.2 jit_solution(7399236186199703974)
XLA Ops:
  0.0 24.9 %shard_map.100 = bf16[16,512]{1,0:T(8,128)(2,1)} custom-call(bf16[16,512]{1,0:T(8,128)(2,1)} %cand_hbm.1, s32[1,16]{1,0:T(1,128)} %bitcast.5, bf16[2048,512]{1,0:T(8,128)(2,1)} %ev_hbm.1, s32[1,2048]{1,0:T(1,128)} %bitcast.3, s32[1,2048]{1,0:T(1,128)} %bitcast.4, bf16[512,512]{1,0:T(8,128)(2,1)} %wq_hbm.1, bf16[512,512]{1,0:T(8,128)(2,1)} %wk_hbm.1, ...), custom_call_target="tpu_custom_call" | custom-call | tf_op jit(solution)/shard_map/pallas_call | solution.py:326
  24.9 1.3 %copy.12 = bf16[16,512]{1,0:T(8,128)(2,1)} copy(bf16[16,512]{1,0:T(8,128)(2,1)} %shard_map.100) | data formatting | bytes 32768

commit v2 on v1

v2 whole, which is shorter than its diff:
```python
import functools
import math

import jax
import jax.numpy as jnp
from jax import lax
from jax.experimental import pallas as pl
from jax.experimental.pallas import tpu as pltpu
from jax.sharding import PartitionSpec as P

HEADS = 4
LANES = 128
FAR = -(2.0**60)
LINK = jnp.bfloat16
F32 = jnp.float32
BF16 = jnp.bfloat16


def divisor(total, wanted):
    return math.gcd(total, wanted)


def kernel(
    n,
    cand_hbm,
    cuser_hbm,
    ev_hbm,
    euser_hbm,
    emask_hbm,
    wq_hbm,
    wk_hbm,
    wv_hbm,
    wg_hbm,
    wo_hbm,
    out_ref,
    cand,
    cuser,
    ev,
    euser,
    emask,
    wq,
    wkv,
    wg,
    wo,
    q_own,
    q_all,
    users,
    keys,
    vals,
    gate,
    part,
    land,
    in_sem,
    ev_sem,
    q_send,
    q_recv,
    u_send,
    u_recv,
    e_send,
    e_recv,
    r_send,
    r_recv,
):
    rows, width = cand.shape
    half = width // 2
    dh = width // HEADS
    pair = HEADS // 2
    events = ev.shape[1]
    chunk = divisor(events, 512)
    ev_chunks = events // chunk
    half_scale = 0.5 / math.sqrt(dh)

    me = lax.axis_index("users")
    c = lax.rem(me, 2)
    other = 1 - c
    sib_id = me - c + other
    sibling = {"users": sib_id}
    columns = pl.ds(pl.multiple_of(c * half, half), half)

    def peer_of(i):
        return lax.rem(me + i, n)

    small = [
        (cand_hbm, cand),
        (cuser_hbm, cuser),
        (wq_hbm, wq),
        (euser_hbm, euser.at[0]),
        (emask_hbm, emask.at[0]),
        (wk_hbm.at[:, columns], wkv.at[:, pl.ds(0, half)]),
        (wv_hbm.at[:, columns], wkv.at[:, pl.ds(half, half)]),
        (wg_hbm, wg),
        (wo_hbm, wo),
    ]
    copies = [pltpu.make_async_copy(s, d, in_sem.at[i]) for i, (s, d) in enumerate(small)]
    ev_copies = [
        pltpu.make_async_copy(
            ev_hbm.at[pl.ds(j * chunk, chunk)], ev.at[0, pl.ds(j * chunk, chunk)], ev_sem.at[j]
        )
        for j in range(ev_chunks)
    ]

    barrier = pltpu.get_barrier_semaphore()

    @pl.loop(1, n)
    def _(i):
        pl.semaphore_signal(barrier, inc=1, device_id={"users": peer_of(i)})

    for copy in copies[:5]:
        copy.start()
    for copy in ev_copies:
        copy.start()
    for copy in copies[5:]:
        copy.start()

    for copy in copies[:3]:
        copy.wait()
    queries = jnp.dot(cand[...], wq[...], preferred_element_type=F32).astype(BF16)
    for core in range(2):
        q_own[core] = queries[:, core * half : (core + 1) * half]
    q_all[me] = q_own[c]
    users[me] = jnp.zeros((1, LANES), jnp.int32)
    users[me, :, pl.ds(0, rows)] = cuser[...]
    copies[3].wait()
    copies[4].wait()
    for copy in ev_copies:
        copy.wait()

    pl.semaphore_wait(barrier, n - 1)

    def q_copy(i):
        peer = peer_of(i)
        return pltpu.make_async_remote_copy(
            src_ref=q_own.at[lax.rem(peer, 2)],
            dst_ref=q_all.at[me],
            send_sem=q_send.at[peer],
            recv_sem=q_recv.at[me],
            device_id={"users": peer},
        )

    def u_copy(i):
        peer = peer_of(i)
        return pltpu.make_async_remote_copy(
            src_ref=users.at[me],
            dst_ref=users.at[me],
            send_sem=u_send.at[peer],
            recv_sem=u_recv.at[me],
            device_id={"users": peer},
        )

    def q_arrival(i):
        peer = peer_of(i)
        return pltpu.make_async_remote_copy(
            src_ref=q_own.at[0],
            dst_ref=q_all.at[peer],
            send_sem=q_send.at[peer],
            recv_sem=q_recv.at[peer],
            device_id={"users": peer},
        )

    def u_arrival(i):
        peer = peer_of(i)
        return pltpu.make_async_remote_copy(
            src_ref=users.at[me],
            dst_ref=users.at[peer],
            send_sem=u_send.at[peer],
            recv_sem=u_recv.at[peer],
            device_id={"users": peer},
        )

    def event_copy(j):
        at = pl.ds(j * chunk, chunk)
        return pltpu.make_async_remote_copy(
            src_ref=ev.at[0, at],
            dst_ref=ev.at[1, at],
            send_sem=e_send.at[j],
            recv_sem=e_recv.at[j],
            device_id=sibling,
        )

    def tag_copy(ref, j):
        return pltpu.make_async_remote_copy(
            src_ref=ref.at[0],
            dst_ref=ref.at[1],
            send_sem=e_send.at[j],
            recv_sem=e_recv.at[j],
            device_id=sibling,
        )

    handed = [event_copy(j) for j in range(ev_chunks)]
    tags = [tag_copy(euser, ev_chunks), tag_copy(emask, ev_chunks + 1)]
    handed[0].start()

    @pl.loop(1, n)
    def _(i):
        q_copy(i).start()
        u_copy(i).start()

    for copy in tags:
        copy.start()
    for copy in handed[1:]:
        copy.start()

    def keys_and_values(e):
        for j in range(ev_chunks):
            at = pl.ds(j * chunk, chunk)
            if e:
                handed[j].wait_recv()
            both = jnp.dot(ev[e, at, :], wkv[...], preferred_element_type=F32).astype(BF16)
            for h in range(pair):
                keys[h, e, at, pl.ds(0, dh)] = both[:, h * dh : (h + 1) * dh]
            vals[e, at, :] = both[:, half:]

    def mask_columns(e):
        for j in range(ev_chunks):
            at = pl.ds(j * chunk, chunk)
            eff = jnp.where(emask[e, :, at] == 1, euser[e, :, at], -1)
            ids = lax.broadcasted_iota(jnp.int32, (LANES, chunk), 0)
            miss = jnp.where(ids == eff, 0.0, FAR).T.astype(BF16)
            for h in range(pair):
                keys[h, e, at, pl.ds(dh, LANES)] = miss

    copies[5].wait()
    copies[6].wait()
    mask_columns(0)
    keys_and_values(0)

    copies[7].wait()
    pre = 0.5 * jnp.dot(cand[...], wg[...], preferred_element_type=F32)
    gate[...] = pre + pre * jnp.tanh(pre)
    copies[8].wait()

    for copy in tags:
        copy.wait_recv()
    mask_columns(1)
    keys_and_values(1)

    @pl.loop(1, n)
    def _(i):
        q_arrival(i).wait_recv()
        u_arrival(i).wait_recv()

    total = n * rows
    block = divisor(total, 256)
    slots = block // rows

    def attention(g, b):
        at_slots = pl.ds(b * slots, slots)
        q = q_all[at_slots].reshape(block, half)[:, g * dh : (g + 1) * dh]
        shape = (slots, rows, LANES)
        own_lane = lax.broadcasted_iota(jnp.int32, shape, 1) == lax.broadcasted_iota(
            jnp.int32, shape, 2
        )
        spread = jnp.where(own_lane, jnp.broadcast_to(users[at_slots], shape).astype(F32), 0.0)
        user_col = jnp.sum(spread, axis=2, keepdims=True)
        lane_ids = lax.broadcasted_iota(jnp.int32, shape, 2).astype(F32)
        one_hot = jnp.where(lane_ids == user_col, 1.0, 0.0).reshape(block, LANES).astype(BF16)
        q = jnp.concatenate([q, one_hot], axis=1)
        acc = None
        for e in range(2):
            for j in range(ev_chunks):
                at = pl.ds(j * chunk, chunk)
                raw = lax.dot_general(
                    q, keys[g, e, at, :], (((1,), (1,)), ((), ())), preferred_element_type=F32
                )
                s = raw * half_scale
                attn = (s + s * jnp.tanh(s)).astype(BF16)
                term = jnp.dot(
                    attn, vals[e, at, pl.ds(g * dh, dh)], preferred_element_type=F32
                )
                acc = term if acc is None else acc + term
        part[g, at_slots] = acc.reshape(slots, rows, dh).astype(LINK)

    def give(g, i):
        peer = peer_of(i)
        return pltpu.make_async_remote_copy(
            src_ref=part.at[g, peer],
            dst_ref=land.at[g, me],
            send_sem=r_send.at[g, peer],
            recv_sem=r_recv.at[g, me],
            device_id={"users": peer},
        )

    def take(g, i):
        peer = peer_of(i)
        return pltpu.make_async_remote_copy(
            src_ref=part.at[g, peer],
            dst_ref=land.at[g, peer],
            send_sem=r_send.at[g, peer],
            recv_sem=r_recv.at[g, peer],
            device_id={"users": peer},
        )

    for g in range(pair):
        if total == block:
            attention(g, 0)
        else:
            pl.loop(0, total // block)(functools.partial(attention, g))

        @pl.loop(1, n)
        def _(i):
            give(g, i).start()

        land[g, me] = part[g, me]

    @pl.loop(1, n)
    def _(i):
        q_copy(i).wait_send()
        u_copy(i).wait_send()

    for copy in handed + tags:
        copy.wait_send()

    sums = []
    for g in range(pair):

        @pl.loop(1, n)
        def _(i):
            take(g, i).wait_recv()

        landed = land[g].astype(F32).reshape(n // 2, 2, rows, dh)
        sums.append(jnp.sum(landed, axis=0))
    summed = jnp.concatenate([sums[g][core] for core in range(2) for g in range(pair)], axis=1)
    mean = jnp.mean(summed, axis=1, keepdims=True)
    centred = summed - mean
    var = jnp.mean(centred * centred, axis=1, keepdims=True)
    normed = centred / jnp.sqrt(var + 1e-5)
    gated = (normed * gate[...]).astype(BF16)
    out_ref[...] = jnp.dot(gated, wo[...], preferred_element_type=F32)

    for g in range(pair):

        @pl.loop(1, n)
        def _(i):
            give(g, i).wait_send()


def per_device(
    n,
    candidates,
    candidate_user,
    events,
    event_user,
    event_mask,
    query_weight,
    key_weight,
    value_weight,
    gate_weight,
    output_weight,
):
    rows, width = candidates.shape
    count = events.shape[0]
    half = width // 2
    pair = HEADS // 2
    dh = width // HEADS
    chunks = count // divisor(count, 512)
    square = pltpu.VMEM((width, width), BF16)
    dma = pltpu.SemaphoreType.DMA
    delta = pl.pallas_call(
        functools.partial(kernel, n),
        out_shape=jax.ShapeDtypeStruct((rows, width), F32),
        in_specs=[pl.BlockSpec(memory_space=pl.ANY)] * 10,
        out_specs=pl.BlockSpec(memory_space=pltpu.VMEM),
        scratch_shapes=[
            pltpu.VMEM((rows, width), BF16),
            pltpu.VMEM((1, rows), jnp.int32),
            pltpu.VMEM((2, count, width), BF16),
            pltpu.VMEM((2, 1, count), jnp.int32),
            pltpu.VMEM((2, 1, count), jnp.int32),
            square,
            square,
            square,
            square,
            pltpu.VMEM((2, rows, half), BF16),
            pltpu.VMEM((n, rows, half), BF16),
            pltpu.VMEM((n, 1, LANES), jnp.int32),
            pltpu.VMEM((pair, 2, count, dh + LANES), BF16),
            pltpu.VMEM((2, count, half), BF16),
            pltpu.VMEM((rows, width), F32),
            pltpu.VMEM((pair, n, rows, dh), LINK),
            pltpu.VMEM((pair, n, rows, dh), LINK),
            dma((9,)),
            dma((chunks,)),
            dma((n,)),
            dma((n,)),
            dma((n,)),
            dma((n,)),
            dma((chunks + 2,)),
            dma((chunks + 2,)),
            dma((pair, n)),
            dma((pair, n)),
        ],
        compiler_params=pltpu.CompilerParams(
            collective_id=0, has_side_effects=True, vmem_limit_bytes=56 * 2**20
        ),
    )(
        candidates,
        candidate_user.reshape(1, rows),
        events,
        event_user.reshape(1, count),
        event_mask.reshape(1, count),
        query_weight,
        key_weight,
        value_weight,
        gate_weight,
        output_weight,
    )
    return (candidates.astype(F32) + delta).astype(BF16)


def solution(mesh):
    spread = ("parts", "users")
    in_specs = (P(spread, None), P(spread), P(spread, None), P(spread), P(spread)) + (P(),) * 5
    return jax.shard_map(
        functools.partial(per_device, mesh.shape["users"]),
        mesh=mesh,
        in_specs=in_specs,
        out_specs=P(spread, None),
        check_vma=False,
    )
```

time: 26.5 us -> 24.1 us (0.909)
  Pallas kernels: 24.9 us -> 22.5 us
  other arithmetic: 0 us -> 1.37 us
  local copies, waits for them, and re-layouts: 1.32 us -> 0.01 us
    pallas_call x1, Pallas kernels: 24.9 us -> 22.5 us  [per_device(): pl.pallas_call(functools.partial(kernel, n), out_shape=jax.ShapeDtypeStru...]
    convert_element_type x0 -> x1, other arithmetic: none -> 1.37 us  [per_device(): return (candidates.astype(F32) + delta).astype(BF16)]
    unnamed x1 -> x2, local copies, waits for them, and re-layouts: 1.32 us -> 0.01 us
where the time goes in v2:
time: 24.1 us; the launch traced here: 23.9 us
  Pallas kernels  22.5 us (93%)
  other arithmetic  1.37 us (6%)
    pallas_call x1, Pallas kernels, per_device(): pl.pallas_call(functools.partial(kernel, n), out_shape=jax.ShapeDtypeStru...  22.5 us
    convert_element_type x1, other arithmetic, per_device(): return (candidates.astype(F32) + delta).astype(BF16)  1.37 us

profile of v2, /device:TPU:0, one launch (start us, length us, event | category | flops | bytes accessed | tf_op | source)
XLA Modules:
  0.0 23.9 jit_solution(9504854944160727448)
XLA Ops:
  0.0 0.0 copy-start
  0.0 22.5 %shard_map.100 = f32[16,512]{1,0:T(8,128)} custom-call(bf16[16,512]{1,0:T(8,128)(2,1)} %cand_hbm.1, s32[1,16]{1,0:T(1,128)} %bitcast.5, bf16[2048,512]{1,0:T(8,128)(2,1)} %ev_hbm.1, s32[1,2048]{1,0:T(1,128)} %bitcast.3, s32[1,2048]{1,0:T(1,128)} %bitcast.4, bf16[512,512]{1,0:T(8,128)(2,1)} %wq_hbm.1, bf16[512,512]{1,0:T(8,128)(2,1)} %wk_hbm.1, ...), custom_call_target="tpu_custom_call" | custom-call | tf_op jit(solution)/shard_map/pallas_call | solution.py:358
  22.5 0.0 copy-done
  22.5 1.4 %add_convert_fusion = bf16[16,512]{1,0:T(8,128)(2,1)} fusion(f32[16,512]{1,0:T(8,128)} %shard_map.100, bf16[16,512]{1,0:T(8,128)(2,1)S(1)} %copy-done), kind=kLoop, calls=%fused_computation | loop fusion | flops 24576 | bytes 65536 | tf_op jit(solution)/shard_map/convert_element_type | solution.py:407
Async XLA Ops:
  0.0 22.5 %copy-start = (bf16[16,512]{1,0:T(8,128)(2,1)S(1)}, bf16[16,512]{1,0:T(8,128)(2,1)}, u32[]{:S(2)}) copy-start(bf16[16,512]{1,0:T(8,128)(2,1)} %cand_hbm.1) | copy-start | bytes 49156

commit v3 on v2

--- a/solution.py
+++ b/solution.py
@@ -18,6 +18,14 @@
 
 def divisor(total, wanted):
     return math.gcd(total, wanted)
+
+
+def each_peer(n, body):
+    if n <= 32:
+        for i in sorted(range(1, n), key=lambda i: abs(i - n // 2)):
+            body(i)
+    else:
+        pl.loop(1, n)(body)
 
 
 def kernel(
@@ -45,6 +53,7 @@
     q_own,
     q_all,
     users,
+    hot,
     keys,
     vals,
     gate,
@@ -101,9 +110,9 @@
 
     barrier = pltpu.get_barrier_semaphore()
 
-    @pl.loop(1, n)
-    def _(i):
-        pl.semaphore_signal(barrier, inc=1, device_id={"users": peer_of(i)})
+    each_peer(
+        n, lambda i: pl.semaphore_signal(barrier, inc=1, device_id={"users": peer_of(i)})
+    )
 
     for copy in copies[:5]:
         copy.start()
@@ -120,10 +129,6 @@
     q_all[me] = q_own[c]
     users[me] = jnp.zeros((1, LANES), jnp.int32)
     users[me, :, pl.ds(0, rows)] = cuser[...]
-    copies[3].wait()
-    copies[4].wait()
-    for copy in ev_copies:
-        copy.wait()
 
     pl.semaphore_wait(barrier, n - 1)
 
@@ -132,8 +137,8 @@
         return pltpu.make_async_remote_copy(
             src_ref=q_own.at[lax.rem(peer, 2)],
             dst_ref=q_all.at[me],
-            send_sem=q_send.at[peer],
-            recv_sem=q_recv.at[me],
+            send_sem=q_send.at[0],
+            recv_sem=q_recv.at[0],
             device_id={"users": peer},
         )
 
@@ -142,30 +147,23 @@
         return pltpu.make_async_remote_copy(
             src_ref=users.at[me],
             dst_ref=users.at[me],
-            send_sem=u_send.at[peer],
-            recv_sem=u_recv.at[me],
+            send_sem=u_send.at[0],
+            recv_sem=u_recv.at[0],
             device_id={"users": peer},
         )
 
-    def q_arrival(i):
-        peer = peer_of(i)
-        return pltpu.make_async_remote_copy(
-            src_ref=q_own.at[0],
-            dst_ref=q_all.at[peer],
-            send_sem=q_send.at[peer],
-            recv_sem=q_recv.at[peer],
-            device_id={"users": peer},
-        )
-
-    def u_arrival(i):
-        peer = peer_of(i)
-        return pltpu.make_async_remote_copy(
-            src_ref=users.at[me],
-            dst_ref=users.at[peer],
-            send_sem=u_send.at[peer],
-            recv_sem=u_recv.at[peer],
-            device_id={"users": peer},
-        )
+    def all_of(ref, send_sem, recv_sem):
+        block = ref.at[pl.ds(0, n - 1)]
+        return pltpu.make_async_remote_copy(
+            src_ref=block,
+            dst_ref=block,
+            send_sem=send_sem,
+            recv_sem=recv_sem,
+            device_id=sibling,
+        )
+
+    all_q = all_of(q_all, q_send.at[0], q_recv.at[0])
+    all_u = all_of(users, u_send.at[0], u_recv.at[0])
 
     def event_copy(j):
         at = pl.ds(j * chunk, chunk)
@@ -188,17 +186,15 @@
 
     handed = [event_copy(j) for j in range(ev_chunks)]
     tags = [tag_copy(euser, ev_chunks), tag_copy(emask, ev_chunks + 1)]
-    handed[0].start()
-
-    @pl.loop(1, n)
-    def _(i):
-        q_copy(i).start()
-        u_copy(i).start()
-
+    each_peer(n, lambda i: q_copy(i).start())
+    for local, copy in zip(ev_copies, handed):
+        local.wait()
+        copy.start()
+    copies[3].wait()
+    copies[4].wait()
     for copy in tags:
         copy.start()
-    for copy in handed[1:]:
-        copy.start()
+    each_peer(n, lambda i: u_copy(i).start())
 
     def keys_and_values(e):
         for j in range(ev_chunks):
@@ -234,27 +230,34 @@
     mask_columns(1)
     keys_and_values(1)
 
-    @pl.loop(1, n)
-    def _(i):
-        q_arrival(i).wait_recv()
-        u_arrival(i).wait_recv()
-
     total = n * rows
     block = divisor(total, 256)
     slots = block // rows
 
+    all_u.wait_recv()
+
+    def one_hot(b):
+        at_slots = pl.ds(b * slots, slots)
+        shape = (slots, rows, LANES)
+        own_lane = lax.broadcasted_iota(jnp.int32, shape, 1) == lax.broadcasted_iota(
+            jnp.int32, shape, 2
+        )
+        spread = jnp.where(own_lane, jnp.broadcast_to(users[at_slots], shape).astype(F32), 0.0)
+        user_col = jnp.sum(spread, axis=2, keepdims=True)
+        lane_ids = lax.broadcasted_iota(jnp.int32, shape, 2).astype(F32)
+        hot[at_slots] = jnp.where(lane_ids == user_col, 1.0, 0.0).astype(BF16)
+
+    if total == block:
+        one_hot(0)
+    else:
+        pl.loop(0, total // block)(one_hot)
+
+    all_q.wait_recv()
+
     def attention(g, b):
         at_slots = pl.ds(b * slots, slots)
         q = q_all[at_slots].reshape(block, half)[:, g * dh : (g + 1) * dh]
-        shape = (slots, rows, LANES)
-        own_lane = lax.broadcasted_iota(jnp.int32, shape, 1) == lax.broadcasted_iota(
-            jnp.int32, shape, 2
-        )
-        spread = jnp.where(own_lane, jnp.broadcast_to(users[at_slots], shape).astype(F32), 0.0)
-        user_col = jnp.sum(spread, axis=2, keepdims=True)
-        lane_ids = lax.broadcasted_iota(jnp.int32, shape, 2).astype(F32)
-        one_hot = jnp.where(lane_ids == user_col, 1.0, 0.0).reshape(block, LANES).astype(BF16)
-        q = jnp.concatenate([q, one_hot], axis=1)
+        q = jnp.concatenate([q, hot[at_slots].reshape(block, LANES)], axis=1)
         acc = None
         for e in range(2):
             for j in range(ev_chunks):
@@ -275,20 +278,12 @@
         return pltpu.make_async_remote_copy(
             src_ref=part.at[g, peer],
             dst_ref=land.at[g, me],
-            send_sem=r_send.at[g, peer],
-            recv_sem=r_recv.at[g, me],
+            send_sem=r_send.at[g],
+            recv_sem=r_recv.at[g],
             device_id={"users": peer},
         )
 
-    def take(g, i):
-        peer = peer_of(i)
-        return pltpu.make_async_remote_copy(
-            src_ref=part.at[g, peer],
-            dst_ref=land.at[g, peer],
-            send_sem=r_send.at[g, peer],
-            recv_sem=r_recv.at[g, peer],
-            device_id={"users": peer},
-        )
+    given = [all_of(land.at[g], r_send.at[g], r_recv.at[g]) for g in range(pair)]
 
     for g in range(pair):
         if total == block:
@@ -296,27 +291,17 @@
         else:
             pl.loop(0, total // block)(functools.partial(attention, g))
 
-        @pl.loop(1, n)
-        def _(i):
-            give(g, i).start()
-
+        each_peer(n, functools.partial(lambda g, i: give(g, i).start(), g))
         land[g, me] = part[g, me]
 
-    @pl.loop(1, n)
-    def _(i):
-        q_copy(i).wait_send()
-        u_copy(i).wait_send()
-
+    all_q.wait_send()
+    all_u.wait_send()
     for copy in handed + tags:
         copy.wait_send()
 
     sums = []
     for g in range(pair):
-
-        @pl.loop(1, n)
-        def _(i):
-            take(g, i).wait_recv()
-
+        given[g].wait_recv()
         landed = land[g].astype(F32).reshape(n // 2, 2, rows, dh)
         sums.append(jnp.sum(landed, axis=0))
     summed = jnp.concatenate([sums[g][core] for core in range(2) for g in range(pair)], axis=1)
@@ -327,11 +312,8 @@
     gated = (normed * gate[...]).astype(BF16)
     out_ref[...] = jnp.dot(gated, wo[...], preferred_element_type=F32)
 
-    for g in range(pair):
-
-        @pl.loop(1, n)
-        def _(i):
-            give(g, i).wait_send()
+    for copy in given:
+        copy.wait_send()
 
 
 def per_device(
@@ -373,6 +355,7 @@
             pltpu.VMEM((2, rows, half), BF16),
             pltpu.VMEM((n, rows, half), BF16),
             pltpu.VMEM((n, 1, LANES), jnp.int32),
+            pltpu.VMEM((n, rows, LANES), BF16),
             pltpu.VMEM((pair, 2, count, dh + LANES), BF16),
             pltpu.VMEM((2, count, half), BF16),
             pltpu.VMEM((rows, width), F32),
@@ -380,14 +363,14 @@
             pltpu.VMEM((pair, n, rows, dh), LINK),
             dma((9,)),
             dma((chunks,)),
-            dma((n,)),
-            dma((n,)),
-            dma((n,)),
-            dma((n,)),
+            dma((1,)),
+            dma((1,)),
+            dma((1,)),
+            dma((1,)),
             dma((chunks + 2,)),
             dma((chunks + 2,)),
-            dma((pair, n)),
-            dma((pair, n)),
+            dma((pair,)),
+            dma((pair,)),
         ],
         compiler_params=pltpu.CompilerParams(
             collective_id=0, has_side_effects=True, vmem_limit_bytes=56 * 2**20

time: 24.1 us -> 23.1 us (0.959)
  Pallas kernels: 22.5 us -> 21.6 us
    pallas_call x1, Pallas kernels: 22.5 us -> 21.6 us  [per_device(): pl.pallas_call(functools.partial(kernel, n), out_shape=jax.ShapeDtypeStru...]
where the time goes in v3:
time: 23.1 us; the launch traced here: 22.9 us
  Pallas kernels  21.6 us (94%)
  other arithmetic  1.37 us (6%)
    pallas_call x1, Pallas kernels, per_device(): pl.pallas_call(functools.partial(kernel, n), out_shape=jax.ShapeDtypeStru...  21.6 us
    convert_element_type x1, other arithmetic, per_device(): return (candidates.astype(F32) + delta).astype(BF16)  1.37 us

profile of v3, /device:TPU:0, one launch (start us, length us, event | category | flops | bytes accessed | tf_op | source)
XLA Modules:
  0.0 22.9 jit_solution(17209249737117333037)
XLA Ops:
  0.0 0.0 copy-start
  0.0 21.6 %shard_map.100 = f32[16,512]{1,0:T(8,128)} custom-call(bf16[16,512]{1,0:T(8,128)(2,1)} %cand_hbm.1, s32[1,16]{1,0:T(1,128)} %bitcast.5, bf16[2048,512]{1,0:T(8,128)(2,1)} %ev_hbm.1, s32[1,2048]{1,0:T(1,128)} %bitcast.3, s32[1,2048]{1,0:T(1,128)} %bitcast.4, bf16[512,512]{1,0:T(8,128)(2,1)} %wq_hbm.1, bf16[512,512]{1,0:T(8,128)(2,1)} %wk_hbm.1, ...), custom_call_target="tpu_custom_call" | custom-call | tf_op jit(solution)/shard_map/pallas_call | solution.py:340
  21.6 0.0 copy-done
  21.6 1.4 %add_convert_fusion = bf16[16,512]{1,0:T(8,128)(2,1)} fusion(f32[16,512]{1,0:T(8,128)} %shard_map.100, bf16[16,512]{1,0:T(8,128)(2,1)S(1)} %copy-done), kind=kLoop, calls=%fused_computation | loop fusion | flops 24576 | bytes 65536 | tf_op jit(solution)/shard_map/convert_element_type | solution.py:390
Async XLA Ops:
  0.0 21.6 %copy-start = (bf16[16,512]{1,0:T(8,128)(2,1)S(1)}, bf16[16,512]{1,0:T(8,128)(2,1)}, u32[]{:S(2)}) copy-start(bf16[16,512]{1,0:T(8,128)(2,1)} %cand_hbm.1) | copy-start | bytes 49156

commit v4 on v3

--- a/solution.py
+++ b/solution.py
@@ -57,6 +57,7 @@
     keys,
     vals,
     gate,
+    own,
     part,
     land,
     in_sem,
@@ -196,8 +197,8 @@
         copy.start()
     each_peer(n, lambda i: u_copy(i).start())
 
-    def keys_and_values(e):
-        for j in range(ev_chunks):
+    def keys_and_values(e, chunks):
+        for j in chunks:
             at = pl.ds(j * chunk, chunk)
             if e:
                 handed[j].wait_recv()
@@ -218,7 +219,8 @@
     copies[5].wait()
     copies[6].wait()
     mask_columns(0)
-    keys_and_values(0)
+    early = ev_chunks // 2
+    keys_and_values(0, range(ev_chunks))
 
     copies[7].wait()
     pre = 0.5 * jnp.dot(cand[...], wg[...], preferred_element_type=F32)
@@ -228,7 +230,7 @@
     for copy in tags:
         copy.wait_recv()
     mask_columns(1)
-    keys_and_values(1)
+    keys_and_values(1, range(early))
 
     total = n * rows
     block = divisor(total, 256)
@@ -254,24 +256,31 @@
 
     all_q.wait_recv()
 
-    def attention(g, b):
+    def attention(g, e, b):
         at_slots = pl.ds(b * slots, slots)
         q = q_all[at_slots].reshape(block, half)[:, g * dh : (g + 1) * dh]
         q = jnp.concatenate([q, hot[at_slots].reshape(block, LANES)], axis=1)
         acc = None
-        for e in range(2):
-            for j in range(ev_chunks):
-                at = pl.ds(j * chunk, chunk)
-                raw = lax.dot_general(
-                    q, keys[g, e, at, :], (((1,), (1,)), ((), ())), preferred_element_type=F32
-                )
-                s = raw * half_scale
-                attn = (s + s * jnp.tanh(s)).astype(BF16)
-                term = jnp.dot(
-                    attn, vals[e, at, pl.ds(g * dh, dh)], preferred_element_type=F32
-                )
-                acc = term if acc is None else acc + term
-        part[g, at_slots] = acc.reshape(slots, rows, dh).astype(LINK)
+        for j in range(ev_chunks):
+            at = pl.ds(j * chunk, chunk)
+            raw = lax.dot_general(
+                q, keys[g, e, at, :], (((1,), (1,)), ((), ())), preferred_element_type=F32
+            )
+            s = raw * half_scale
+            attn = (s + s * jnp.tanh(s)).astype(BF16)
+            term = jnp.dot(attn, vals[e, at, pl.ds(g * dh, dh)], preferred_element_type=F32)
+            acc = term if acc is None else acc + term
+        acc = acc.reshape(slots, rows, dh)
+        if e:
+            part[g, at_slots] = (own[g, at_slots] + acc).astype(LINK)
+        else:
+            own[g, at_slots] = acc
+
+    def attend(g, e):
+        if total == block:
+            attention(g, e, 0)
+        else:
+            pl.loop(0, total // block)(functools.partial(attention, g, e))
 
     def give(g, i):
         peer = peer_of(i)
@@ -286,11 +295,10 @@
     given = [all_of(land.at[g], r_send.at[g], r_recv.at[g]) for g in range(pair)]
 
     for g in range(pair):
-        if total == block:
-            attention(g, 0)
-        else:
-            pl.loop(0, total // block)(functools.partial(attention, g))
-
+        attend(g, 0)
+    keys_and_values(1, range(early, ev_chunks))
+    for g in range(pair):
+        attend(g, 1)
         each_peer(n, functools.partial(lambda g, i: give(g, i).start(), g))
         land[g, me] = part[g, me]
 
@@ -359,6 +367,7 @@
             pltpu.VMEM((pair, 2, count, dh + LANES), BF16),
             pltpu.VMEM((2, count, half), BF16),
             pltpu.VMEM((rows, width), F32),
+            pltpu.VMEM((pair, n, rows, dh), F32),
             pltpu.VMEM((pair, n, rows, dh), LINK),
             pltpu.VMEM((pair, n, rows, dh), LINK),
             dma((9,)),

time: 23.1 us -> 23.9 us (1.035)
  Pallas kernels: 21.6 us -> 22.3 us
    pallas_call x1, Pallas kernels: 21.6 us -> 22.3 us  [per_device(): pl.pallas_call(functools.partial(kernel, n), out_shape=jax.ShapeDtypeStru...]
where the time goes in v4:
time: 23.9 us; the launch traced here: 23.7 us
  Pallas kernels  22.3 us (93%)
  other arithmetic  1.37 us (6%)
    pallas_call x1, Pallas kernels, per_device(): pl.pallas_call(functools.partial(kernel, n), out_shape=jax.ShapeDtypeStru...  22.3 us
    convert_element_type x1, other arithmetic, per_device(): return (candidates.astype(F32) + delta).astype(BF16)  1.37 us

profile of v4, /device:TPU:0, one launch (start us, length us, event | category | flops | bytes accessed | tf_op | source)
XLA Modules:
  0.0 23.7 jit_solution(13903872440884636261)
XLA Ops:
  0.0 0.0 copy-start
  0.0 22.3 %shard_map.100 = f32[16,512]{1,0:T(8,128)} custom-call(bf16[16,512]{1,0:T(8,128)(2,1)} %cand_hbm.1, s32[1,16]{1,0:T(1,128)} %bitcast.5, bf16[2048,512]{1,0:T(8,128)(2,1)} %ev_hbm.1, s32[1,2048]{1,0:T(1,128)} %bitcast.3, s32[1,2048]{1,0:T(1,128)} %bitcast.4, bf16[512,512]{1,0:T(8,128)(2,1)} %wq_hbm.1, bf16[512,512]{1,0:T(8,128)(2,1)} %wk_hbm.1, ...), custom_call_target="tpu_custom_call" | custom-call | tf_op jit(solution)/shard_map/pallas_call | solution.py:348
  22.3 0.0 copy-done
  22.3 1.4 %add_convert_fusion = bf16[16,512]{1,0:T(8,128)(2,1)} fusion(f32[16,512]{1,0:T(8,128)} %shard_map.100, bf16[16,512]{1,0:T(8,128)(2,1)S(1)} %copy-done), kind=kLoop, calls=%fused_computation | loop fusion | flops 24576 | bytes 65536 | tf_op jit(solution)/shard_map/convert_element_type | solution.py:399
Async XLA Ops:
  0.0 22.3 %copy-start = (bf16[16,512]{1,0:T(8,128)(2,1)S(1)}, bf16[16,512]{1,0:T(8,128)(2,1)}, u32[]{:S(2)}) copy-start(bf16[16,512]{1,0:T(8,128)(2,1)} %cand_hbm.1) | copy-start | bytes 49156

commit v5 on v3

--- a/solution.py
+++ b/solution.py
@@ -187,6 +187,7 @@
     handed = [event_copy(j) for j in range(ev_chunks)]
     tags = [tag_copy(euser, ev_chunks), tag_copy(emask, ev_chunks + 1)]
     each_peer(n, lambda i: q_copy(i).start())
+    each_peer(n, lambda i: u_copy(i).start())
     for local, copy in zip(ev_copies, handed):
         local.wait()
         copy.start()
@@ -194,7 +195,6 @@
     copies[4].wait()
     for copy in tags:
         copy.start()
-    each_peer(n, lambda i: u_copy(i).start())
 
     def keys_and_values(e):
         for j in range(ev_chunks):

time: 23.1 us -> 23.1 us (level)
  no operation moved by 1% of the time
where the time goes in v5:
time: 23.1 us; the launch traced here: 22.9 us
  Pallas kernels  21.6 us (94%)
  other arithmetic  1.37 us (6%)
    pallas_call x1, Pallas kernels, per_device(): pl.pallas_call(functools.partial(kernel, n), out_shape=jax.ShapeDtypeStru...  21.6 us
    convert_element_type x1, other arithmetic, per_device(): return (candidates.astype(F32) + delta).astype(BF16)  1.37 us

profile of v5, /device:TPU:0, one launch (start us, length us, event | category | flops | bytes accessed | tf_op | source)
XLA Modules:
  0.0 22.9 jit_solution(17220673335494134441)
XLA Ops:
  0.0 0.0 copy-start
  0.0 21.6 %shard_map.100 = f32[16,512]{1,0:T(8,128)} custom-call(bf16[16,512]{1,0:T(8,128)(2,1)} %cand_hbm.1, s32[1,16]{1,0:T(1,128)} %bitcast.5, bf16[2048,512]{1,0:T(8,128)(2,1)} %ev_hbm.1, s32[1,2048]{1,0:T(1,128)} %bitcast.3, s32[1,2048]{1,0:T(1,128)} %bitcast.4, bf16[512,512]{1,0:T(8,128)(2,1)} %wq_hbm.1, bf16[512,512]{1,0:T(8,128)(2,1)} %wk_hbm.1, ...), custom_call_target="tpu_custom_call" | custom-call | tf_op jit(solution)/shard_map/pallas_call | solution.py:340
  21.6 0.0 copy-done
  21.6 1.4 %add_convert_fusion = bf16[16,512]{1,0:T(8,128)(2,1)} fusion(f32[16,512]{1,0:T(8,128)} %shard_map.100, bf16[16,512]{1,0:T(8,128)(2,1)S(1)} %copy-done), kind=kLoop, calls=%fused_computation | loop fusion | flops 24576 | bytes 65536 | tf_op jit(solution)/shard_map/convert_element_type | solution.py:390
Async XLA Ops:
  0.0 21.6 %copy-start = (bf16[16,512]{1,0:T(8,128)(2,1)S(1)}, bf16[16,512]{1,0:T(8,128)(2,1)}, u32[]{:S(2)}) copy-start(bf16[16,512]{1,0:T(8,128)(2,1)} %cand_hbm.1) | copy-start | bytes 49156
